TPU v7x, 256 devices: a whole 4x4x8 slice. The times are simulated.
256 devices in a mesh: ma: 64 (over y, z_hi, x, core), af: 4 (over z_lo).
Axes of the slice: x: 4, y: 4, z: 8 (z_hi: 2, z_lo: 4; z = z_hi * 4 + z_lo), core: 2. Of those that a mesh axis runs over, the one named last changes fastest.
Arguments:
- visibilities: bfloat16 [2, 2, 4096, 32640], P(None, None, 'ma', 'af'), may hold values from -6 to 6
- pair_base: int32 [32640], P('af'), may hold values from 0 to 8191, as said below
- window_starts: int32 [64], replicated, may hold values from 0 to 4080
- beam: bfloat16 [2, 1024, 2, 32, 8192], P(None, 'ma', None, None, 'af'), may hold values from -0.046875 to 0.046875
- kl_basis: float32 [1024, 128, 128], P(('ma', 'af')), may hold values from -0.5 to 0.5
Outputs:
- kl_modes: float32 [1024, 128], P(('ma', 'af'))
Inputs may be any that keep to these rules, and one draw needn't show every extreme that they name: `pair_base`: pairs in the k-th aligned block of 8160 pairs name only baselines of the k-th block of 2048 baselines, and every baseline is named by at least one pair.
All inputs are finite; a program needn't handle non-finite values.
Results may differ from a plain program's by a relative error of at most 0.0046.
Values may be sent and summed in bfloat16 or wider, within the bound.
A program may use at most 128 MiB of HBM per device.

v0:
```python
import math

import jax
import jax.numpy as jnp
from jax import lax
from jax.sharding import PartitionSpec as P

TIMES = 4096
M_SEG = 16


TWO_PI = 2.0 * math.pi


def dft_table(window_starts, length, seg_len):
    within = lax.iota(jnp.int32, seg_len)
    mode_ids = (window_starts[:, None] + within[None, :]).reshape(-1)
    sample_ids = lax.iota(jnp.int32, length)
    phase = sample_ids[:, None] * mode_ids[None, :] % length
    angle = phase.astype(jnp.float32) * (TWO_PI / length)
    scale_factor = 1.0 / math.sqrt(length)
    cosine = jnp.cos(angle) * scale_factor
    sine = jnp.sin(angle) * scale_factor
    return jnp.concatenate([cosine, sine], axis=1).astype(jnp.bfloat16)


def transform(series, dft_tab):
    base_count = series.shape[0]
    chan_count = series.shape[1]
    length = series.shape[3]
    flat_rows = series.reshape(base_count * chan_count * 2, length)
    product = jnp.dot(flat_rows, dft_tab, preferred_element_type=jnp.float32)
    mode_count = product.shape[1] // 2
    product = product.reshape(base_count, chan_count, 2, 2, mode_count)
    real_part = product[:, :, 0, 0] + product[:, :, 1, 1]
    imag_part = product[:, :, 1, 0] - product[:, :, 0, 1]
    return jnp.stack([real_part, imag_part], axis=2).astype(jnp.bfloat16)


def body(visibilities, pair_base, window_starts, beam, kl_basis):
    chan_count = visibilities.shape[0]
    time_local = visibilities.shape[2]
    pair_local = visibilities.shape[3]
    base_local = beam.shape[4]
    block_size = math.gcd(512, base_local)
    local_ids = pair_base - lax.axis_index("af") * base_local
    flat_rows = visibilities.reshape(chan_count * 2 * time_local, pair_local)

    def compress(start):
        wanted = start + lax.iota(jnp.int32, block_size)
        matches = local_ids[:, None] == wanted[None, :]
        counts = jnp.sum(matches.astype(jnp.float32), axis=0)
        totals = lax.dot_general(
            matches.astype(jnp.bfloat16),
            flat_rows,
            (((0,), (1,)), ((), ())),
            preferred_element_type=jnp.float32,
        )
        return (totals / counts[:, None]).astype(jnp.bfloat16)

    starts = lax.iota(jnp.int32, base_local // block_size) * block_size
    compressed = lax.map(compress, starts).reshape(base_local, chan_count, 2, time_local)
    dft_tab = dft_table(window_starts, TIMES, M_SEG)
    series = lax.all_to_all(compressed, "ma", split_axis=0, concat_axis=3, tiled=True)
    spectra = transform(series, dft_tab)
    regrouped = lax.all_to_all(spectra, "ma", split_axis=3, concat_axis=0, tiled=True)
    paired = jnp.einsum("cmqsb,bcrm->mcqsr", beam, regrouped, preferred_element_type=jnp.float32)
    real_sky = paired[:, :, 0, :, 0] + paired[:, :, 1, :, 1]
    imag_sky = paired[:, :, 0, :, 1] - paired[:, :, 1, :, 0]
    partial_sky = jnp.stack([real_sky, imag_sky], axis=2)
    whole_sky = lax.psum(partial_sky, "af")
    share_rows = whole_sky.shape[0] // lax.axis_size("af")
    sky_part = lax.dynamic_slice_in_dim(whole_sky, lax.axis_index("af") * share_rows, share_rows, 0)
    vectors = sky_part.reshape(sky_part.shape[0], -1)
    return jnp.einsum("mkv,mv->mk", kl_basis, vectors, precision=lax.Precision.HIGHEST)


def solution(mesh):
    in_specs = (
        P(None, None, "ma", "af"),
        P("af"),
        P(),
        P(None, "ma", None, None, "af"),
        P(("ma", "af"), None, None),
    )
    out_specs = P(("ma", "af"), None)
    return jax.shard_map(body, mesh=mesh, in_specs=in_specs, out_specs=out_specs, check_vma=False)
```

profile of v0, /device:TPU:1, one launch (start us, length us, event | category | flops | bytes accessed | tf_op | source)
XLA Modules:
  0.0 210.9 jit_solution(4821255338759073467)
XLA Ops:
  0.8 42.0 %while.10 = (s32[]{:T(128)}, bf16[4,512,256]{2,1,0:T(8,128)(2,1)S(1)}, s32[8160]{0:T(1024)S(1)}, s32[4]{0:T(128)S(1)}, bf16[256,8160]{1,0:T(8,128)(2,1)}, /*index=5*/s32[]{:T(128)}) while((s32[]{:T(128)}, bf16[4,512,256]{2,1,0:T(8,128)(2,1)S(1)}, s32[8160]{0:T(1024)S(1)}, s32[4]{0:T(128)S(1)}, bf16[256,8160]{1,0:T(8,128)(2,1)}, ...), condition=%wide.region_2.3_spmd, body=%wide.region_0.2_spmd.sunk | while | flops 2160246784 | bytes 4515801 | solution.py:62
  2.1 3.6 %fusion.37 = f32[512]{0:T(512)S(1)} fusion(s32[512]{0:T(512)S(1)} %iota_add_fusion.3, s32[8160]{0:T(1024)S(1)} %get-tuple-element.93), kind=kLoop, calls=%fused_computation.2.clone.1 | loop fusion | flops 12533248 | bytes 36736 | tf_op jit(solution)/shard_map/while/body/eval_jaxpr/reduce_sum | solution.py:52
  5.6 5.7 %fusion.38 = bf16[4,512,256]{2,1,0:T(8,128)(2,1)S(1)} fusion(bf16[4,512,256]{2,1,0:T(8,128)(2,1)S(1)} %get-tuple-element.86, s32[]{:T(128)} %get-tuple-element.85, bf16[256,8160]{1,0:T(8,128)(2,1)} %get-tuple-element.95, s32[512]{0:T(512)S(1)} %iota_add_fusion.3, s32[8160]{0:T(1024)S(1)} %get-tuple-element.93, f32[512]{0:T(512)S(1)} %fusion.37), kind=kOutput, calls=%fused_computation.9.clone.1 | convolution fusion | flops 2147713024 | bytes 4476932 | tf_op jit(solution)/shard_map/while/body/eval_jaxpr/dot_general | solution.py:53
  12.6 3.6 %fusion.37 = f32[512]{0:T(512)S(1)} fusion(s32[512]{0:T(512)S(1)} %iota_add_fusion.3, s32[8160]{0:T(1024)S(1)} %get-tuple-element.93), kind=kLoop, calls=%fused_computation.2.clone.1 | loop fusion | flops 12533248 | bytes 36736 | tf_op jit(solution)/shard_map/while/body/eval_jaxpr/reduce_sum | solution.py:52
  16.1 5.7 %fusion.38 = bf16[4,512,256]{2,1,0:T(8,128)(2,1)S(1)} fusion(bf16[4,512,256]{2,1,0:T(8,128)(2,1)S(1)} %get-tuple-element.86, s32[]{:T(128)} %get-tuple-element.85, bf16[256,8160]{1,0:T(8,128)(2,1)} %get-tuple-element.95, s32[512]{0:T(512)S(1)} %iota_add_fusion.3, s32[8160]{0:T(1024)S(1)} %get-tuple-element.93, f32[512]{0:T(512)S(1)} %fusion.37), kind=kOutput, calls=%fused_computation.9.clone.1 | convolution fusion | flops 2147713024 | bytes 4476932 | tf_op jit(solution)/shard_map/while/body/eval_jaxpr/dot_general | solution.py:53
  23.1 3.6 %fusion.37 = f32[512]{0:T(512)S(1)} fusion(s32[512]{0:T(512)S(1)} %iota_add_fusion.3, s32[8160]{0:T(1024)S(1)} %get-tuple-element.93), kind=kLoop, calls=%fused_computation.2.clone.1 | loop fusion | flops 12533248 | bytes 36736 | tf_op jit(solution)/shard_map/while/body/eval_jaxpr/reduce_sum | solution.py:52
  26.6 5.7 %fusion.38 = bf16[4,512,256]{2,1,0:T(8,128)(2,1)S(1)} fusion(bf16[4,512,256]{2,1,0:T(8,128)(2,1)S(1)} %get-tuple-element.86, s32[]{:T(128)} %get-tuple-element.85, bf16[256,8160]{1,0:T(8,128)(2,1)} %get-tuple-element.95, s32[512]{0:T(512)S(1)} %iota_add_fusion.3, s32[8160]{0:T(1024)S(1)} %get-tuple-element.93, f32[512]{0:T(512)S(1)} %fusion.37), kind=kOutput, calls=%fused_computation.9.clone.1 | convolution fusion | flops 2147713024 | bytes 4476932 | tf_op jit(solution)/shard_map/while/body/eval_jaxpr/dot_general | solution.py:53
  33.6 3.6 %fusion.37 = f32[512]{0:T(512)S(1)} fusion(s32[512]{0:T(512)S(1)} %iota_add_fusion.3, s32[8160]{0:T(1024)S(1)} %get-tuple-element.93), kind=kLoop, calls=%fused_computation.2.clone.1 | loop fusion | flops 12533248 | bytes 36736 | tf_op jit(solution)/shard_map/while/body/eval_jaxpr/reduce_sum | solution.py:52
  37.1 5.7 %fusion.38 = bf16[4,512,256]{2,1,0:T(8,128)(2,1)S(1)} fusion(bf16[4,512,256]{2,1,0:T(8,128)(2,1)S(1)} %get-tuple-element.86, s32[]{:T(128)} %get-tuple-element.85, bf16[256,8160]{1,0:T(8,128)(2,1)} %get-tuple-element.95, s32[512]{0:T(512)S(1)} %iota_add_fusion.3, s32[8160]{0:T(1024)S(1)} %get-tuple-element.93, f32[512]{0:T(512)S(1)} %fusion.37), kind=kOutput, calls=%fused_computation.9.clone.1 | convolution fusion | flops 2147713024 | bytes 4476932 | tf_op jit(solution)/shard_map/while/body/eval_jaxpr/dot_general | solution.py:53
  42.9 0.9 reshape.118
  43.7 2.3 %reshape.123 = bf16[64,2,4096]{2,1,0:T(2,128)(2,1)} reshape(bf16[2048,2,2,64]{3,2,1,0:T(2,128)(2,1)S(1)} %reshape.118) | data formatting | bytes 2097152
  46.0 15.6 %all-to-all-start = ((bf16[64,2,4096]{2,1,0:T(2,128)(2,1)}), bf16[64,2,4096]{2,1,0:T(2,128)(2,1)S(1)}, u32[]{:S(2)}, u32[]{:S(2)}) async-start(bf16[64,2,4096]{2,1,0:T(2,128)(2,1)} %reshape.123), calls=%async_computation | async-start | bytes 2097152 | tf_op jit(solution)/shard_map/all_to_all | solution.py:64
  61.8 69.4 %multiply_convert_fusion.1 = (bf16[4096,1024]{0,1:T(8,128)(2,1)S(1)}, bf16[4096,1024]{0,1:T(8,128)(2,1)S(1)}) fusion(s32[1024]{0:T(1024)S(1)} %add.73), kind=kLoop, calls=%fused_computation.19 | loop fusion | flops 75497472 | bytes 16781312 | tf_op jit(solution)/shard_map/convert.4
  131.2 7.2 %pad_maximum_fusion = bf16[4096,2048]{0,1:T(8,128)(2,1)} fusion(bf16[4096,1024]{0,1:T(8,128)(2,1)S(1)} %get-tuple-element.47, bf16[4096,1024]{0,1:T(8,128)(2,1)S(1)} %get-tuple-element.46), kind=kLoop, calls=%fused_computation.17 | loop fusion | flops 33554432 | bytes 33554432 | tf_op jit(solution)/shard_map/concatenate | solution.py:24
  138.4 1.3 reshape.124
  140.9 1.7 reshape.113
  142.5 11.4 %fusion.19 = f32[32,2,2,2,1024]{4,0,3,2,1:T(8,128)S(1)} fusion(bf16[2,1024,4096,1,1]{2,1,0,4,3:T(8,128)(2,1)} %bitcast.73, bf16[32,2,2,4096,1]{3,0,2,1,4:T(8,128)(2,1)S(1)} %reshape.113), kind=kOutput, calls=%fused_computation.26 | convolution fusion | flops 2147483648 | bytes 18874368 | tf_op jit(solution)/shard_map/dot_general | solution.py:32
  154.8 1.7 reshape.125
  156.5 12.8 %all-to-all-start.1 = ((bf16[64,2,1024]{2,1,0:T(2,128)(2,1)}), bf16[64,2,1024]{2,1,0:T(2,128)(2,1)S(1)}, u32[]{:S(2)}, u32[]{:S(2)}) async-start(bf16[64,2,1024]{2,1,0:T(2,128)(2,1)} %reshape.125), calls=%async_computation.1 | async-start | bytes 524288 | tf_op jit(solution)/shard_map/all_to_all | solution.py:66
  169.3 13.8 %all-to-all-done.1 = bf16[64,2,1024]{2,1,0:T(2,128)(2,1)S(1)} async-done(((bf16[64,2,1024]{2,1,0:T(2,128)(2,1)}), bf16[64,2,1024]{2,1,0:T(2,128)(2,1)S(1)}, u32[]{:S(2)}, u32[]{:S(2)}) %all-to-all-start.1) | async-done | bytes 262176 | tf_op jit(solution)/shard_map/all_to_all | solution.py:66
  184.0 1.0 reshape.115
  185.0 8.9 %fusion.16 = f32[16,2,2,32,2]{3,4,2,1,0:T(2,128)S(1)} fusion(bf16[2,16,2,32,2048]{4,3,2,1,0:T(8,128)(2,1)} %param.10, bf16[2048,2,2,16,1]{0,2,1,3,4:T(2,128)(2,1)S(1)} %reshape.115), kind=kOutput, calls=%fused_computation.25 | convolution fusion | flops 16777216 | bytes 8667136 | tf_op jit(solution)/shard_map/cmqsb,bcrm->mcqsr/dot_general | solution.py:67
  194.0 15.7 %psum.7 = f32[16,2,2,32]{3,1,0,2:T(2,128)S(1)} all-reduce(f32[16,2,2,32]{3,1,0,2:T(2,128)S(1)} %pad_maximum_fusion.2), channel_id=1, replica_groups=mesh['ma'=64,'af'=4] {'af'}, use_global_device_ids=true, to_apply=%region_3.4 | all-reduce | flops 2048 | bytes 16384 | tf_op jit(solution)/shard_map/psum | solution.py:71
  209.8 1.1 fusion.28
  (33 shorter events, 8.9 us)
Async XLA Ops:
  0.0 209.8 %copy-start = (f32[4,128,128]{2,1,0:T(8,128)S(1)}, f32[4,128,128]{2,1,0:T(8,128)}, u32[]{:S(2)}) copy-start(f32[4,128,128]{2,1,0:T(8,128)} %param.11) | copy-start | bytes 786436
  0.8 60.8 %copy-start.1 = (s32[64]{0:T(128)S(1)}, s32[64]{0:T(128)}, u32[]{:S(2)}) copy-start(s32[64]{0:T(128)} %param.9) | copy-start | bytes 772
  46.0 92.4 %all-to-all-start = ((bf16[64,2,4096]{2,1,0:T(2,128)(2,1)}), bf16[64,2,4096]{2,1,0:T(2,128)(2,1)S(1)}, u32[]{:S(2)}, u32[]{:S(2)}) async-start(bf16[64,2,4096]{2,1,0:T(2,128)(2,1)} %reshape.123), calls=%async_computation | async-start | bytes 2097152 | tf_op jit(solution)/shard_map/all_to_all | solution.py:64
  156.5 26.5 %all-to-all-start.1 = ((bf16[64,2,1024]{2,1,0:T(2,128)(2,1)}), bf16[64,2,1024]{2,1,0:T(2,128)(2,1)S(1)}, u32[]{:S(2)}, u32[]{:S(2)}) async-start(bf16[64,2,1024]{2,1,0:T(2,128)(2,1)} %reshape.125), calls=%async_computation.1 | async-start | bytes 524288 | tf_op jit(solution)/shard_map/all_to_all | solution.py:66
where the time goes:
time: 213 us; the launch traced here: 211 us
  other arithmetic  94.3 us (44%)
  matrix products  44.2 us (21%)
  starting transfers between devices  28.4 us (13%)
  blocking collectives  15.7 us (7%)
  local copies, waits for them, and re-layouts  14.3 us (7%)
  waiting for transfers between devices  13.8 us (6%)
    another operation x1, other arithmetic  69.4 us
    dot_general x4, matrix products, compress(): lax.dot_general(matches.astype(jnp.bfloat16), flat_rows, (((0,), (1,)), (...  22.8 us
    psum x1, blocking collectives, body(): whole_sky = lax.psum(partial_sky, 'af')  15.7 us
    all_to_all x1, starting transfers between devices, body(): lax.all_to_all(compressed, 'ma', split_axis=0, concat_axis=3, tiled=True)  15.6 us
    reduce_sum x4, other arithmetic, compress(): counts = jnp.sum(matches.astype(jnp.float32), axis=0)  14.2 us
    all_to_all x1, waiting for transfers between devices, body(): lax.all_to_all(spectra, 'ma', split_axis=3, concat_axis=0, tiled=True)  13.8 us
    all_to_all x1, starting transfers between devices, body(): lax.all_to_all(spectra, 'ma', split_axis=3, concat_axis=0, tiled=True)  12.8 us
    dot_general x1, matrix products, transform(): product = jnp.dot(flat_rows, dft_tab, preferred_element_type=jnp.float32)  11.4 us
  transfers between devices with their start and end apart: 2, of which 1 were waited for; matrix products, arithmetic and copies ran while one was open for 36% of the time, Pallas kernels for 0%

commit v1 on v0

v1 whole, which is shorter than its diff:
```python
import functools
import math

import jax
import jax.numpy as jnp
from jax import lax
from jax.experimental import pallas as pl
from jax.experimental.pallas import tpu as pltpu
from jax.sharding import PartitionSpec as P

MESH = pl.DeviceIdType.MESH
F32 = jnp.float32
BF16 = jnp.bfloat16

TIMES = 4096
SEG = 16
SEGS = 64
PAIRS = 8160
PADDED = 8192
WHOLE = 7936
BASES = 2048
T_BLK = 64
HALF = 32
B_BLK = 128
CHUNK = 256
NT = (((1,), (1,)), ((), ()))


def to_ma(half, g):
    return (g // 8) * 16 + half * 8 + g % 8


def sincos(phase):
    quadrant = (phase + 512) >> 10
    x = (phase - (quadrant << 10)).astype(F32) * (2.0 * math.pi / TIMES)
    x2 = x * x
    s = x * (1.0 + x2 * (-1.0 / 6 + x2 * (1.0 / 120 + x2 * (-1.0 / 5040 + x2 * (1.0 / 362880)))))
    c = 1.0 + x2 * (-0.5 + x2 * (1.0 / 24 + x2 * (-1.0 / 720 + x2 * (1.0 / 40320))))
    odd = (quadrant & 1) == 1
    cos = jnp.where(odd, s, c)
    sin = jnp.where(odd, c, s)
    cos = jnp.where(((quadrant + 1) & 2) == 2, -cos, cos)
    sin = jnp.where((quadrant & 2) == 2, -sin, sin)
    return cos, sin


def kernel(
    starts, ids, kl, vis_hbm, beam_hbm, out,
    vis, tail, beam, local, counts, table, s1, r1, s2, r2, weights, total, v_send, v_recv,
    vis_sem, beam_sem, ss1, rs1, ss2, rs2, z_sem, ssv, rsv,
):
    ma = lax.axis_index("ma")
    af = lax.axis_index("af")
    y = ma // 16
    half = (ma // 8) % 2
    g = y * 8 + ma % 8
    partner = to_ma(1 - half, g)

    vis_copy = pltpu.make_async_copy(vis_hbm, vis, vis_sem)
    vis_copy.start()
    beam_copy = pltpu.make_async_copy(beam_hbm, beam, beam_sem)
    beam_copy.start()

    barrier = pltpu.get_barrier_semaphore()
    pl.semaphore_signal(barrier, inc=1, device_id=(partner, af), device_id_type=MESH)

    def greet(k, _):
        pl.semaphore_signal(barrier, inc=1, device_id=(to_ma(half, lax.rem(g + k, HALF)), af), device_id_type=MESH)
        return 0

    lax.fori_loop(1, HALF, greet, 0)

    def greet_af(k, _):
        pl.semaphore_signal(barrier, inc=1, device_id=(ma, lax.rem(af + k, 4)), device_id_type=MESH)
        return 0

    lax.fori_loop(1, 4, greet_af, 0)

    local[...] = jnp.full(local.shape, -1, jnp.int32)
    local[:, pl.ds(0, PAIRS)] = ids[...] - af * BASES
    here = local[...]
    high = (here >> 7).astype(F32)
    low = (here & 127).astype(F32)
    rows_hi = lax.broadcasted_iota(jnp.int32, (16, PADDED), 0).astype(F32)
    rows_lo = lax.broadcasted_iota(jnp.int32, (B_BLK, PADDED), 0).astype(F32)
    one_hi = jnp.where(rows_hi == jnp.broadcast_to(high, (16, PADDED)), 1.0, 0.0).astype(BF16)
    one_lo = jnp.where(rows_lo == jnp.broadcast_to(low, (B_BLK, PADDED)), 1.0, 0.0).astype(BF16)
    counts[...] = lax.dot_general(one_hi, one_lo, NT, preferred_element_type=F32)

    weights[...] = jnp.zeros(weights.shape, BF16)
    v_send[...] = jnp.zeros(v_send.shape, F32)

    vis_copy.wait()
    tail[...] = jnp.zeros(tail.shape, BF16)
    tail[:, pl.ds(0, PAIRS - WHOLE)] = vis[:, pl.ds(WHOLE, PAIRS - WHOLE)]

    def compress(j):
        start = j * CHUNK
        wanted = local[...] - start
        wanted = jnp.where((wanted >= 0) & (wanted < CHUNK), wanted, -1).astype(BF16)
        rows = lax.broadcasted_iota(jnp.int32, (CHUNK, PADDED), 0).astype(BF16)
        one = jnp.where(rows == jnp.broadcast_to(wanted, (CHUNK, PADDED)), BF16(1), BF16(0))
        sums = lax.dot_general(vis[:, pl.ds(0, WHOLE)], one[:, :WHOLE], NT, preferred_element_type=F32)
        sums += lax.dot_general(tail[...], one[:, WHOLE:], NT, preferred_element_type=F32)
        for h in range(2):
            scale = 1.0 / counts[pl.ds(j * 2 + h, 1), :]
            for c in range(2):
                for r in range(2):
                    piece = sums[(c * 2 + r) * T_BLK : (c * 2 + r + 1) * T_BLK, h * B_BLK : (h + 1) * B_BLK]
                    s1[j * 4 + h * 2 + c, :, r * B_BLK : (r + 1) * B_BLK] = (piece * scale).astype(BF16)

    def send_block(d):
        @pl.when(d == g)
        def _():
            pltpu.make_async_copy(s1.at[d], r1.at[d], rs1.at[y]).start()

        @pl.when(d != g)
        def _():
            pltpu.make_async_remote_copy(
                src_ref=s1.at[d], dst_ref=r1.at[g], send_sem=ss1, recv_sem=rs1.at[y],
                device_id=(to_ma(half, d), af), device_id_type=MESH,
            ).start()

    first = g // 4

    def send_chunk(j):
        def one(k, _):
            send_block(j * 4 + k)
            return 0

        lax.fori_loop(0, 4, one, 0)

    compress(first)
    pl.semaphore_wait(barrier, HALF - 1 + 1 + 3)
    pl.semaphore_signal(z_sem, inc=1, device_id=(partner, af), device_id_type=MESH)
    send_chunk(first)

    def chunk_step(k, _):
        j = lax.rem(first + k, 8)
        compress(j)
        send_chunk(j)
        return 0

    lax.fori_loop(1, 8, chunk_step, 0)

    lanes = lax.broadcasted_iota(jnp.int32, (SEG, 128), 1)
    within = lax.broadcasted_iota(jnp.int32, (SEG, 128), 0)
    blk_time = (lanes // 4) * 1024 + half * 512 + (lanes % 4) * 128

    def table_step(s, _):
        mode = starts[s] + within
        base_c, base_s = sincos((lanes * mode) & (TIMES - 1))
        base_c = base_c * (1.0 / math.sqrt(TIMES))
        base_s = base_s * (1.0 / math.sqrt(TIMES))
        blk_c, blk_s = sincos((blk_time * mode) & (TIMES - 1))
        row = pl.multiple_of(s * SEG, SEG)
        for b in range(16):
            c = jnp.broadcast_to(blk_c[:, b : b + 1], (SEG, 128))
            d = jnp.broadcast_to(blk_s[:, b : b + 1], (SEG, 128))
            table[pl.ds(row, SEG), b * 128 : (b + 1) * 128] = (base_c * c - base_s * d).astype(BF16)
            table[pl.ds(row + SEGS * SEG, SEG), b * 128 : (b + 1) * 128] = (base_s * c + base_c * d).astype(BF16)
        return 0

    lax.fori_loop(0, SEGS, table_step, 0)

    for q in range(4):
        part = r1.at[pl.ds(q * 8, 8)]
        pltpu.make_async_copy(part, part, rs1.at[q]).wait()
    pl.semaphore_wait(z_sem, 1)

    def transform_step(k, _):
        tile = lax.rem(y + k, 4)
        row = pl.multiple_of(tile * 256, 256)
        series = r1[...].reshape(HALF * T_BLK, 2 * B_BLK)
        along_cos = jnp.dot(table[pl.ds(row, 256), :], series, preferred_element_type=F32)
        along_sin = jnp.dot(table[pl.ds(row + 1024, 256), :], series, preferred_element_type=F32)
        real = along_cos[:, :B_BLK] + along_sin[:, B_BLK:]
        imag = along_cos[:, B_BLK:] - along_sin[:, :B_BLK]
        s2[pl.ds(tile * 16, 16), :, 0:B_BLK] = real.astype(BF16).reshape(16, SEG, B_BLK)
        s2[pl.ds(tile * 16, 16), :, B_BLK : 2 * B_BLK] = imag.astype(BF16).reshape(16, SEG, B_BLK)

        def send(i, _):
            d = tile * 16 + lax.rem(i + (1 - half) * 8, 16)

            @pl.when(d == ma)
            def _():
                pltpu.make_async_copy(s2.at[d], r2.at[d], rs2.at[y]).start()

            @pl.when(d != ma)
            def _():
                pltpu.make_async_remote_copy(
                    src_ref=s2.at[d], dst_ref=r2.at[ma], send_sem=ss2, recv_sem=rs2.at[y],
                    device_id=(d, af), device_id_type=MESH,
                ).start()

            return 0

        lax.fori_loop(0, 16, send, 0)
        return 0

    lax.fori_loop(0, 4, transform_step, 0)

    beam_copy.wait()

    def project_step(k, _):
        q = lax.rem(y - k + 4, 4)
        part = r2.at[pl.ds(q * 16, 16)]
        pltpu.make_async_copy(part, part, rs2.at[q]).wait()
        for c in range(2):
            for h in range(2):
                for x in range(4):
                    block = r2[q * 16 + h * 8 + x * 2 + c]
                    for r in range(2):
                        weights[c, (h * 2 + r) * SEG : (h * 2 + r + 1) * SEG, x * B_BLK : (x + 1) * B_BLK] = block[:, r * B_BLK : (r + 1) * B_BLK]
        column = pl.multiple_of(q * 512, 512)
        for c in range(2):
            got = lax.dot_general(beam[c, :, pl.ds(column, 512)], weights[c], NT, preferred_element_type=F32)

            @pl.when(k == 0)
            def _():
                total[c] = got

            @pl.when(k != 0)
            def _():
                total[c] += got

        return 0

    lax.fori_loop(0, 4, project_step, 0)

    lane = lax.broadcasted_iota(jnp.int32, (32, 128), 1)
    is_real = ((lane >> 4) & 1) == 0
    pieces = []
    for c in range(2):
        own = []
        for q in range(2):
            kept = jnp.zeros((32, 128), F32)
            for m in range(SEG):
                kept = jnp.where((lane & 15) == m, total[c, m * 64 + q * 32 : m * 64 + (q + 1) * 32, :], kept)
            own.append(kept)
        pieces.append(jnp.where(is_real, own[0], own[1]))
        pieces.append(jnp.where(is_real, -own[1], own[0]))
    turned = jnp.concatenate(pieces, axis=0).T
    sky = turned[0:16] + turned[16:32] + turned[32:48] + turned[48:64]
    for a in range(4):
        v_send[a, 0:4, :] = sky[a * 4 : a * 4 + 4]
    pltpu.make_async_copy(v_send.at[af], v_recv.at[af], rsv).start()

    def send_sky(k, _):
        a = lax.rem(af + k, 4)
        pltpu.make_async_remote_copy(
            src_ref=v_send.at[a], dst_ref=v_recv.at[af], send_sem=ssv, recv_sem=rsv,
            device_id=(ma, a), device_id_type=MESH,
        ).start()
        return 0

    lax.fori_loop(1, 4, send_sky, 0)
    pltpu.make_async_copy(v_recv, v_recv, rsv).wait()
    vectors = v_recv[0] + v_recv[1] + v_recv[2] + v_recv[3]
    for m in range(4):
        product = kl[m] * jnp.broadcast_to(vectors[m : m + 1, :], (128, 128))
        out[m : m + 1, :] = jnp.sum(product.T, axis=0, keepdims=True)

    sent = s1.at[pl.ds(0, HALF - 1)]
    pltpu.make_async_copy(sent, sent, ss1).wait()
    sent = s2.at[pl.ds(0, SEGS - 1)]
    pltpu.make_async_copy(sent, sent, ss2).wait()
    sent = v_send.at[pl.ds(0, 3)]
    pltpu.make_async_copy(sent, sent, ssv).wait()


def body(visibilities, pair_base, window_starts, beam, kl_basis):
    vis = visibilities.reshape(4 * T_BLK, PAIRS)
    rows = beam.reshape(2, SEG * 64, BASES)
    vmem = pl.BlockSpec(memory_space=pltpu.VMEM)
    return pl.pallas_call(
        kernel,
        out_shape=jax.ShapeDtypeStruct((4, 128), F32),
        in_specs=[
            pl.BlockSpec(memory_space=pltpu.SMEM),
            vmem,
            vmem,
            pl.BlockSpec(memory_space=pl.ANY),
            pl.BlockSpec(memory_space=pl.ANY),
        ],
        out_specs=vmem,
        scratch_shapes=[
            pltpu.VMEM((4 * T_BLK, PAIRS), BF16),
            pltpu.VMEM((4 * T_BLK, PADDED - WHOLE), BF16),
            pltpu.VMEM((2, SEG * 64, BASES), BF16),
            pltpu.VMEM((1, PADDED), jnp.int32),
            pltpu.VMEM((16, B_BLK), F32),
            pltpu.VMEM((2 * SEGS * SEG, HALF * T_BLK), BF16),
            pltpu.VMEM((HALF, T_BLK, 2 * B_BLK), BF16),
            pltpu.VMEM((HALF, T_BLK, 2 * B_BLK), BF16),
            pltpu.VMEM((SEGS, SEG, 2 * B_BLK), BF16),
            pltpu.VMEM((SEGS, SEG, 2 * B_BLK), BF16),
            pltpu.VMEM((2, 128, 512), BF16),
            pltpu.VMEM((2, SEG * 64, 128), F32),
            pltpu.VMEM((4, 8, 128), F32),
            pltpu.VMEM((4, 8, 128), F32),
            pltpu.SemaphoreType.DMA,
            pltpu.SemaphoreType.DMA,
            pltpu.SemaphoreType.DMA,
            pltpu.SemaphoreType.DMA((4,)),
            pltpu.SemaphoreType.DMA,
            pltpu.SemaphoreType.DMA((4,)),
            pltpu.SemaphoreType.REGULAR,
            pltpu.SemaphoreType.DMA,
            pltpu.SemaphoreType.DMA,
        ],
        compiler_params=pltpu.CompilerParams(
            collective_id=0, has_side_effects=True, vmem_limit_bytes=56 * 2**20
        ),
    )(window_starts, pair_base.reshape(1, PAIRS), kl_basis, vis, rows)


def solution(mesh):
    in_specs = (
        P(None, None, "ma", "af"),
        P("af"),
        P(),
        P(None, "ma", None, None, "af"),
        P(("ma", "af"), None, None),
    )
    out_specs = P(("ma", "af"), None)
    return jax.shard_map(body, mesh=mesh, in_specs=in_specs, out_specs=out_specs, check_vma=False)
```

time: 213 us -> 58 us (0.27)
  other arithmetic: 94.3 us -> 0 us
  Pallas kernels: 0 us -> 56.6 us
  matrix products: 44.2 us -> 0 us
  starting transfers between devices: 28.4 us -> 0 us
  blocking collectives: 15.7 us -> 0 us
  waiting for transfers between devices: 13.8 us -> 0 us
  local copies, waits for them, and re-layouts: 14.3 us -> 1.26 us
    another operation x3 -> x0, other arithmetic: 69.4 us -> none
    pallas_call x0 -> x1, Pallas kernels: none -> 56.6 us  [body(): pl.pallas_call(kernel, out_shape=jax.ShapeDtypeStruct((4, 128), F32), in_...]
    dot_general x7 -> x0, matrix products: 44.2 us -> none  [the longest x4 22.8 us: compress(): lax.dot_general(matches.astype(jnp.bfloat16), flat_rows, (((0,), (1,)), (...]
    all_to_all x2 -> x0, starting transfers between devices: 28.4 us -> none  [the longest x1 15.6 us: body(): lax.all_to_all(compressed, 'ma', split_axis=0, concat_axis=3, tiled=True)]
    psum x1 -> x0, blocking collectives: 15.7 us -> none  [body(): whole_sky = lax.psum(partial_sky, 'af')]
    reduce_sum x4 -> x0, other arithmetic: 14.2 us -> none  [compress(): counts = jnp.sum(matches.astype(jnp.float32), axis=0)]
    all_to_all x2 -> x0, waiting for transfers between devices: 13.8 us -> none  [the longest x1 13.8 us: body(): lax.all_to_all(spectra, 'ma', split_axis=3, concat_axis=0, tiled=True)]
    concatenate x1 -> x0, other arithmetic: 7.23 us -> none  [dft_table(): return jnp.concatenate([cosine, sine], axis=1).astype(jnp.bfloat16)]
  transfers between devices with their start and end apart: 2 -> 0, of which waited for: 1 -> 0; matrix products, arithmetic and copies ran while one was open for 36% -> 0% of each run, Pallas kernels for 0% -> 0%
where the time goes in v1:
time: 58 us; the launch traced here: 57.9 us
  Pallas kernels  56.6 us (98%)
  local copies, waits for them, and re-layouts  1.26 us (2%)
    pallas_call x1, Pallas kernels, body(): pl.pallas_call(kernel, out_shape=jax.ShapeDtypeStruct((4, 128), F32), in_...  56.6 us
    unnamed x1, local copies, waits for them, and re-layouts  1.26 us

profile of v1, /device:TPU:1, one launch (start us, length us, event | category | flops | bytes accessed | tf_op | source)
XLA Modules:
  0.0 57.9 jit_solution(15031355038637044626)
XLA Ops:
  0.0 56.6 %shard_map.55 = f32[4,128]{1,0:T(4,128)} custom-call(s32[64]{0:T(128)} %starts.1, s32[1,8160]{1,0:T(1,128)} %bitcast.5, f32[4,128,128]{2,1,0:T(8,128)} %kl.1, bf16[256,8160]{1,0:T(8,128)(2,1)} %bitcast.4, bf16[2,1024,2048]{2,1,0:T(8,128)(2,1)} %bitcast.3), custom_call_target="tpu_custom_call" | custom-call | tf_op jit(solution)/shard_map/pallas_call | solution.py:276
  56.6 1.3 %copy.7 = f32[4,128]{1,0:T(4,128)} copy(f32[4,128]{1,0:T(4,128)} %shard_map.55) | data formatting | bytes 4096

commit v2 on v1

v2 whole, which is shorter than its diff:
```python
import math

import jax
import jax.numpy as jnp
from jax import lax
from jax.experimental import pallas as pl
from jax.experimental.pallas import tpu as pltpu
from jax.sharding import PartitionSpec as P

MESH = pl.DeviceIdType.MESH
F32 = jnp.float32
BF16 = jnp.bfloat16

TIMES = 4096
SEG = 16
SEGS = 64
PAIRS = 8160
PADDED = 8192
WHOLE = 7936
BASES = 2048
T_BLK = 64
HALF = 32
B_BLK = 64
CHUNK = 256
OFFSETS = (
    ((2, 1), (2, 3), (1, 2), (3, 2)),
    ((2, 0), (0, 2), (1, 1), (3, 3)),
    ((1, 3), (3, 1), (2, 2), (1, 0)),
    ((0, 1), (3, 0), (0, 3), (0, 0)),
)
NT = (((1,), (1,)), ((), ()))


def to_ma(half, g):
    return (g // 8) * 16 + half * 8 + g % 8


def sincos(phase):
    quadrant = (phase + 512) >> 10
    x = (phase - (quadrant << 10)).astype(F32) * (2.0 * math.pi / TIMES)
    x2 = x * x
    s = x * (1.0 + x2 * (-1.0 / 6 + x2 * (1.0 / 120 + x2 * (-1.0 / 5040 + x2 * (1.0 / 362880)))))
    c = 1.0 + x2 * (-0.5 + x2 * (1.0 / 24 + x2 * (-1.0 / 720 + x2 * (1.0 / 40320))))
    odd = (quadrant & 1) == 1
    cos = jnp.where(odd, s, c)
    sin = jnp.where(odd, c, s)
    cos = jnp.where(((quadrant + 1) & 2) == 2, -cos, cos)
    sin = jnp.where((quadrant & 2) == 2, -sin, sin)
    return cos, sin


def kernel(
    starts, ids, kl, vis_hbm, beam_hbm, out,
    vis, tail, beam, high, low, counts, table, s1, r1, s2, r2, series, halves, weights, total, turned_kl, v_send, v_recv,
    vis_sem, beam_sem, ss1, rs1, ss2, rs2, z_sem, ssv, rsv,
):
    ma = lax.axis_index("ma")
    af = lax.axis_index("af")
    y = ma // 16
    half = (ma // 8) % 2
    g = y * 8 + ma % 8
    x = (g // 2) % 4
    partner = to_ma(1 - half, g)

    vis_copy = pltpu.make_async_copy(vis_hbm, vis, vis_sem)
    vis_copy.start()

    barrier = pltpu.get_barrier_semaphore()
    pl.semaphore_signal(barrier, inc=1, device_id=(partner, af), device_id_type=MESH)

    def greet(k, _):
        pl.semaphore_signal(barrier, inc=1, device_id=(to_ma(half, lax.rem(g + k, HALF)), af), device_id_type=MESH)
        return 0

    lax.fori_loop(1, HALF, greet, 0)

    def greet_af(k, _):
        pl.semaphore_signal(barrier, inc=1, device_id=(ma, lax.rem(af + k, 4)), device_id_type=MESH)
        return 0

    lax.fori_loop(1, 4, greet_af, 0)

    high[...] = jnp.full(high.shape, -1, jnp.int32)
    low[...] = jnp.zeros(low.shape, F32)
    local = ids[...] - af * BASES
    high[:, pl.ds(0, PAIRS)] = local >> 6
    low[:, pl.ds(0, PAIRS)] = (local & 63).astype(F32)
    rows_hi = lax.broadcasted_iota(jnp.int32, (32, PADDED), 0)
    rows_lo = (lax.broadcasted_iota(jnp.int32, (2 * B_BLK, PADDED), 0) & (B_BLK - 1)).astype(BF16)
    one_hi = jnp.where(rows_hi == jnp.broadcast_to(high[...], (32, PADDED)), 1.0, 0.0).astype(BF16)
    one_lo = jnp.where(rows_lo == jnp.broadcast_to(low[...].astype(BF16), (2 * B_BLK, PADDED)), BF16(1), BF16(0))
    counts[...] = lax.dot_general(one_hi, one_lo, NT, preferred_element_type=F32)

    lanes = lax.broadcasted_iota(jnp.int32, (SEG, 128), 1)
    within = lax.broadcasted_iota(jnp.int32, (SEG, 128), 0)

    def table_step(step):
        k = step // 16
        tile = step % 16
        start = jnp.full((SEG, 128), 0, jnp.int32)
        for w in range(4):
            start = jnp.where((within >> 2) == w, starts[tile * 4 + w], start)
        mode = start + ((k - start) & 3) + 4 * (within & 3)
        cos, sin = sincos(((lanes + half * 512) * mode) & (TIMES - 1))
        cos = cos * (1.0 / math.sqrt(TIMES))
        sin = sin * (1.0 / math.sqrt(TIMES))
        step_c, step_s = sincos((128 * mode) & (TIMES - 1))
        row = pl.multiple_of(tile * SEG, SEG)
        for b in range(4):
            table[k, pl.ds(row, SEG), b * 128 : (b + 1) * 128] = cos.astype(BF16)
            table[k, pl.ds(row + 256, SEG), b * 128 : (b + 1) * 128] = sin.astype(BF16)
            if b < 3:
                cos, sin = cos * step_c - sin * step_s, sin * step_c + cos * step_s

    def table_steps(i, _):
        for w in range(4):
            table_step(i * 4 + w)
        return 0

    lax.fori_loop(0, 16, table_steps, 0)

    vis_copy.wait()
    beam_copy = pltpu.make_async_copy(beam_hbm, beam, beam_sem)
    beam_copy.start()
    tail[...] = jnp.zeros(tail.shape, BF16)
    tail[:, pl.ds(0, PAIRS - WHOLE)] = vis[:, pl.ds(WHOLE, PAIRS - WHOLE)]

    lane = lax.broadcasted_iota(jnp.int32, (1, 128), 1)
    left = lane < B_BLK

    def chunk_step(k, _):
        batch = k // 4
        n = k % 4
        chips = []
        for sub in range(4):
            dx = dy = 0
            for i in range(4):
                dx = jnp.where(n == i, OFFSETS[i][sub][0], dx)
                dy = jnp.where(n == i, OFFSETS[i][sub][1], dy)
            chips.append(lax.rem(y + dy, 4) * 4 + lax.rem(x + dx, 4))
        wanted = jnp.full((1, PADDED), -1.0, F32)
        for sub in range(4):
            wanted = jnp.where(high[...] == batch * 16 + chips[sub], low[...] + (sub * B_BLK), wanted)
        rows = lax.broadcasted_iota(jnp.int32, (CHUNK, PADDED), 0).astype(BF16)
        one = jnp.where(rows == jnp.broadcast_to(wanted.astype(BF16), (CHUNK, PADDED)), BF16(1), BF16(0))
        sums = lax.dot_general(vis[:, pl.ds(0, WHOLE)], one[:, :WHOLE], NT, preferred_element_type=F32)
        sums += lax.dot_general(tail[...], one[:, WHOLE:], NT, preferred_element_type=F32)
        for pair in range(2):
            near, far = chips[pair * 2], chips[pair * 2 + 1]
            scale = 1.0 / jnp.where(left, counts[pl.ds(batch * 16 + near, 1), :], counts[pl.ds(batch * 16 + far, 1), :])
            for c in range(2):
                real = sums[c * 128 : c * 128 + T_BLK, pair * 128 : (pair + 1) * 128] * scale
                imag = sums[c * 128 + T_BLK : (c + 1) * 128, pair * 128 : (pair + 1) * 128] * scale
                s1[batch, near * 2 + c] = jnp.where(left, real, pltpu.roll(imag, B_BLK, 1)).astype(BF16)
                s1[batch, far * 2 + c] = jnp.where(left, pltpu.roll(real, B_BLK, 1), imag).astype(BF16)

        @pl.when(k == 0)
        def _():
            pl.semaphore_wait(barrier, HALF - 1 + 1 + 3)
            pl.semaphore_signal(z_sem, inc=1, device_id=(partner, af), device_id_type=MESH)

        for sub in range(4):
            for c in range(2):
                d = chips[sub] * 2 + c

                @pl.when(d == g)
                def _():
                    pltpu.make_async_copy(s1.at[batch, d], r1.at[batch, d], rs1.at[batch]).start()

                @pl.when(d != g)
                def _():
                    pltpu.make_async_remote_copy(
                        src_ref=s1.at[batch, d], dst_ref=r1.at[batch, g], send_sem=ss1, recv_sem=rs1.at[batch],
                        device_id=(to_ma(half, d), af), device_id_type=MESH,
                    ).start()

        return 0

    sign = jnp.where(left, 1.0, -1.0)
    upper = (lax.broadcasted_iota(jnp.int32, (1, 8, 1), 1)) < 4

    def transform(batch, _):
        part = r1.at[batch]
        pltpu.make_async_copy(part, part, rs1.at[batch]).wait()
        a = [r1[batch, q * 8 : (q + 1) * 8].reshape(8 * T_BLK, 2 * B_BLK).astype(F32) for q in range(4)]
        even, odd = a[0] + a[2], a[1] + a[3]
        series[0] = (even + odd).astype(BF16)
        series[2] = (even - odd).astype(BF16)
        even, odd = a[0] - a[2], sign * pltpu.roll(a[1] - a[3], B_BLK, 1)
        series[1] = (even + odd).astype(BF16)
        series[3] = (even - odd).astype(BF16)
        both = []
        for k in range(4):
            along = jnp.dot(table[k], series[k], preferred_element_type=F32)
            mixed = along[0:256] + sign * pltpu.roll(along[256:512], B_BLK, 1)
            both.append(mixed.reshape(32, 8, 2 * B_BLK))
        for p in range(2):
            first, second = both[2 * p], both[2 * p + 1]
            now = jnp.where(upper, first, pltpu.roll(second, 4, 1))
            later = jnp.where(upper, pltpu.roll(first, 4, 1), second)
            halves[:, 0, p * 8 : (p + 1) * 8, :] = now
            halves[:, 1, p * 8 : (p + 1) * 8, :] = later
        s2[batch] = halves[...].reshape(SEGS, SEG, 2 * B_BLK).astype(BF16)

        def send(i, _):
            d = lax.rem(y + i // 16, 4) * 16 + lax.rem(i % 16 + (1 - half) * 8, 16)

            @pl.when(d == ma)
            def _():
                pltpu.make_async_copy(s2.at[batch, d], r2.at[batch, d], rs2.at[batch, y]).start()

            @pl.when(d != ma)
            def _():
                pltpu.make_async_remote_copy(
                    src_ref=s2.at[batch, d], dst_ref=r2.at[batch, ma], send_sem=ss2, recv_sem=rs2.at[batch, y],
                    device_id=(d, af), device_id_type=MESH,
                ).start()

            return 0

        lax.fori_loop(0, SEGS, send, 0)
        return 0

    lax.fori_loop(0, 8, chunk_step, 0)
    pl.semaphore_wait(z_sem, 1)
    lax.fori_loop(0, 2, transform, 0)
    for m in range(4):
        turned_kl[m] = kl[m].T
    weights[...] = jnp.zeros(weights.shape, BF16)
    total[...] = jnp.zeros(total.shape, F32)
    v_send[...] = jnp.zeros(v_send.shape, F32)


    beam_copy.wait()

    def project_step(k, _):
        batch = k // 4
        q = lax.rem(y - k % 4 + 4, 4)
        part = r2.at[batch, pl.ds(q * 16, 16)]
        pltpu.make_async_copy(part, part, rs2.at[batch, q]).wait()
        for c in range(2):
            for h in range(2):
                for pair in range(2):
                    near = r2[batch, q * 16 + h * 8 + pair * 4 + c].astype(F32)
                    far = r2[batch, q * 16 + h * 8 + pair * 4 + 2 + c].astype(F32)
                    real = jnp.where(left, near, pltpu.roll(far, B_BLK, 1))
                    imag = jnp.where(left, pltpu.roll(near, B_BLK, 1), far)
                    weights[c, h * 2 * SEG : (h * 2 + 1) * SEG, pair * 128 : (pair + 1) * 128] = real.astype(BF16)
                    weights[c, (h * 2 + 1) * SEG : (h * 2 + 2) * SEG, pair * 128 : (pair + 1) * 128] = imag.astype(BF16)
        column = pl.multiple_of(batch * 1024 + q * 256, 256)
        for c in range(2):
            total[c] += lax.dot_general(beam[c, :, pl.ds(column, 256)], weights[c], NT, preferred_element_type=F32)
        return 0

    lax.fori_loop(0, 8, project_step, 0)

    mode_lane = lax.broadcasted_iota(jnp.int32, (32, 128), 1)
    is_real = ((mode_lane >> 4) & 1) == 0
    mode_of = ((((mode_lane >> 2) & 3) - starts[ma]) & 3) + 4 * (mode_lane & 3)
    pieces = []
    for c in range(2):
        own = []
        for q in range(2):
            kept = jnp.zeros((32, 128), F32)
            for m in range(SEG):
                kept = jnp.where(mode_of == m, total[c, m * 64 + q * 32 : m * 64 + (q + 1) * 32, :], kept)
            own.append(kept)
        pieces.append(jnp.where(is_real, own[0], own[1]))
        pieces.append(jnp.where(is_real, -own[1], own[0]))
    turned = jnp.concatenate(pieces, axis=0).T
    sky = turned[0:16] + turned[16:32] + turned[32:48] + turned[48:64]
    window = jnp.full((4, 128), 0, jnp.int32) + starts[ma]
    for i in range(4):
        kept = sky[0:4]
        for k in range(1, 4):
            kept = jnp.where(((window + i) & 3) == k, sky[k * 4 : k * 4 + 4], kept)
        for n in range(4):
            v_send[n, i : i + 1, :] = kept[n : n + 1]
    pltpu.make_async_copy(v_send.at[af], v_recv.at[af], rsv).start()

    def send_sky(k, _):
        a = lax.rem(af + k, 4)
        pltpu.make_async_remote_copy(
            src_ref=v_send.at[a], dst_ref=v_recv.at[af], send_sem=ssv, recv_sem=rsv,
            device_id=(ma, a), device_id_type=MESH,
        ).start()
        return 0

    lax.fori_loop(1, 4, send_sky, 0)
    pltpu.make_async_copy(v_recv, v_recv, rsv).wait()
    vectors = (v_recv[0] + v_recv[1] + v_recv[2] + v_recv[3]).T
    for m in range(4):
        product = turned_kl[m] * jnp.broadcast_to(vectors[:, m : m + 1], (128, 128))
        out[m : m + 1, :] = jnp.sum(product, axis=0, keepdims=True)

    sent = s1.at[:, pl.ds(0, HALF - 1)]
    pltpu.make_async_copy(sent, sent, ss1).wait()
    sent = s2.at[:, pl.ds(0, SEGS - 1)]
    pltpu.make_async_copy(sent, sent, ss2).wait()
    sent = v_send.at[pl.ds(0, 3)]
    pltpu.make_async_copy(sent, sent, ssv).wait()


def body(visibilities, pair_base, window_starts, beam, kl_basis):
    vis = visibilities.reshape(4 * T_BLK, PAIRS)
    rows = beam.reshape(2, SEG * 64, BASES)
    vmem = pl.BlockSpec(memory_space=pltpu.VMEM)
    return pl.pallas_call(
        kernel,
        out_shape=pltpu.VMEM((4, 128), F32),
        in_specs=[
            pl.BlockSpec(memory_space=pltpu.SMEM),
            vmem,
            vmem,
            pl.BlockSpec(memory_space=pl.ANY),
            pl.BlockSpec(memory_space=pl.ANY),
        ],
        out_specs=vmem,
        scratch_shapes=[
            pltpu.VMEM((4 * T_BLK, PAIRS), BF16),
            pltpu.VMEM((4 * T_BLK, PADDED - WHOLE), BF16),
            pltpu.VMEM((2, SEG * 64, BASES), BF16),
            pltpu.VMEM((1, PADDED), jnp.int32),
            pltpu.VMEM((1, PADDED), F32),
            pltpu.VMEM((32, 2 * B_BLK), F32),
            pltpu.VMEM((4, 512, 512), BF16),
            pltpu.VMEM((2, HALF, T_BLK, 2 * B_BLK), BF16),
            pltpu.VMEM((2, HALF, T_BLK, 2 * B_BLK), BF16),
            pltpu.VMEM((2, SEGS, SEG, 2 * B_BLK), BF16),
            pltpu.VMEM((2, SEGS, SEG, 2 * B_BLK), BF16),
            pltpu.VMEM((4, 512, 2 * B_BLK), BF16),
            pltpu.VMEM((SEGS // 2, 2, SEG, 2 * B_BLK), F32),
            pltpu.VMEM((2, 128, 256), BF16),
            pltpu.VMEM((2, SEG * 64, 128), F32),
            pltpu.VMEM((4, 128, 128), F32),
            pltpu.VMEM((4, 8, 128), F32),
            pltpu.VMEM((4, 8, 128), F32),
            pltpu.SemaphoreType.DMA,
            pltpu.SemaphoreType.DMA,
            pltpu.SemaphoreType.DMA,
            pltpu.SemaphoreType.DMA((2,)),
            pltpu.SemaphoreType.DMA,
            pltpu.SemaphoreType.DMA((2, 4)),
            pltpu.SemaphoreType.REGULAR,
            pltpu.SemaphoreType.DMA,
            pltpu.SemaphoreType.DMA,
        ],
        compiler_params=pltpu.CompilerParams(
            collective_id=0, has_side_effects=True, vmem_limit_bytes=56 * 2**20
        ),
    )(window_starts, pair_base.reshape(1, PAIRS), kl_basis, vis, rows)


def solution(mesh):
    in_specs = (
        P(None, None, "ma", "af"),
        P("af"),
        P(),
        P(None, "ma", None, None, "af"),
        P(("ma", "af"), None, None),
    )
    out_specs = P(("ma", "af"), None)
    return jax.shard_map(body, mesh=mesh, in_specs=in_specs, out_specs=out_specs, check_vma=False)
```

time: 58 us -> 47.6 us (0.82)
  Pallas kernels: 56.6 us -> 46.9 us
  local copies, waits for them, and re-layouts: 1.26 us -> 0.58 us
    pallas_call x1, Pallas kernels: 56.6 us -> 46.9 us  [body(): pl.pallas_call(kernel, out_shape=pltpu.VMEM((4, 128), F32), in_specs=[pl....]
    unnamed x1, local copies, waits for them, and re-layouts: 1.26 us -> 0.58 us
where the time goes in v2:
time: 47.6 us; the launch traced here: 47.5 us
  Pallas kernels  46.9 us (99%)
  local copies, waits for them, and re-layouts  0.58 us (1%)
    pallas_call x1, Pallas kernels, body(): pl.pallas_call(kernel, out_shape=pltpu.VMEM((4, 128), F32), in_specs=[pl....  46.9 us

profile of v2, /device:TPU:1, one launch (start us, length us, event | category | flops | bytes accessed | tf_op | source)
XLA Modules:
  0.0 47.5 jit_solution(17897346875930463962)
XLA Ops:
  0.0 46.9 %shard_map.55 = f32[4,128]{1,0:T(4,128)S(1)} custom-call(s32[64]{0:T(128)} %starts.1, s32[1,8160]{1,0:T(1,128)} %bitcast.5, f32[4,128,128]{2,1,0:T(8,128)} %kl.1, bf16[256,8160]{1,0:T(8,128)(2,1)} %bitcast.4, bf16[2,1024,2048]{2,1,0:T(8,128)(2,1)} %bitcast.3), custom_call_target="tpu_custom_call" | custom-call | tf_op jit(solution)/shard_map/pallas_call | solution.py:308
  46.9 0.6 %copy.7 = f32[4,128]{1,0:T(4,128)} copy(f32[4,128]{1,0:T(4,128)S(1)} %shard_map.55) | data formatting | bytes 4096

commit v3 on v2

--- a/solution.py
+++ b/solution.py
@@ -50,9 +50,9 @@
 
 
 def kernel(
-    starts, ids, kl, vis_hbm, beam_hbm, out,
-    vis, tail, beam, high, low, counts, table, s1, r1, s2, r2, series, halves, weights, total, turned_kl, v_send, v_recv,
-    vis_sem, beam_sem, ss1, rs1, ss2, rs2, z_sem, ssv, rsv,
+    starts, ids, kl_hbm, vis_hbm, beam_hbm, out,
+    vis, tail, beam, high, low, counts, table, s1, r1, s2, r2, series, halves, weights, total, kl, turned_kl, v_send, v_recv,
+    vis_sem, kl_sem, beam_sem, ss1, rs1, ss2, rs2, z_sem, ssv, rsv,
 ):
     ma = lax.axis_index("ma")
     af = lax.axis_index("af")
@@ -64,6 +64,8 @@
 
     vis_copy = pltpu.make_async_copy(vis_hbm, vis, vis_sem)
     vis_copy.start()
+    kl_copy = pltpu.make_async_copy(kl_hbm, kl, kl_sem)
+    kl_copy.start()
 
     barrier = pltpu.get_barrier_semaphore()
     pl.semaphore_signal(barrier, inc=1, device_id=(partner, af), device_id_type=MESH)
@@ -93,31 +95,41 @@
 
     lanes = lax.broadcasted_iota(jnp.int32, (SEG, 128), 1)
     within = lax.broadcasted_iota(jnp.int32, (SEG, 128), 0)
-
-    def table_step(step):
-        k = step // 16
-        tile = step % 16
+    window_row = within >> 2
+    first_time = lanes + half * 512
+    turns = []
+    for b in range(4):
+        up = sincos((first_time + 128 * b) & (TIMES - 1))
+        down = sincos((-3 * (first_time + 128 * b)) & (TIMES - 1))
+        turns.append((up, down))
+
+    def table_step(tile, _):
         start = jnp.full((SEG, 128), 0, jnp.int32)
         for w in range(4):
-            start = jnp.where((within >> 2) == w, starts[tile * 4 + w], start)
-        mode = start + ((k - start) & 3) + 4 * (within & 3)
-        cos, sin = sincos(((lanes + half * 512) * mode) & (TIMES - 1))
+            start = jnp.where(window_row == w, starts[tile * 4 + w], start)
+        mode = start + ((-start) & 3) + 4 * (within & 3)
+        cos, sin = sincos((first_time * mode) & (TIMES - 1))
         cos = cos * (1.0 / math.sqrt(TIMES))
         sin = sin * (1.0 / math.sqrt(TIMES))
         step_c, step_s = sincos((128 * mode) & (TIMES - 1))
-        row = pl.multiple_of(tile * SEG, SEG)
+        own = jnp.where((tile // 2) % 2 == half, 1, 0)
+        row = pl.multiple_of((tile // 4 * 2 + tile % 2) * SEG, SEG)
+        wraps = [((k - start) & 3) == 0 for k in range(4)]
         for b in range(4):
-            table[k, pl.ds(row, SEG), b * 128 : (b + 1) * 128] = cos.astype(BF16)
-            table[k, pl.ds(row + 256, SEG), b * 128 : (b + 1) * 128] = sin.astype(BF16)
+            c, d = cos, sin
+            for k in range(4):
+                if k:
+                    (up_c, up_s), (down_c, down_s) = turns[b]
+                    turn_c = jnp.where(wraps[k], down_c, up_c)
+                    turn_s = jnp.where(wraps[k], down_s, up_s)
+                    c, d = c * turn_c - d * turn_s, d * turn_c + c * turn_s
+                table[k, own, pl.ds(row, SEG), b * 128 : (b + 1) * 128] = c.astype(BF16)
+                table[k, own, pl.ds(row + 128, SEG), b * 128 : (b + 1) * 128] = d.astype(BF16)
             if b < 3:
                 cos, sin = cos * step_c - sin * step_s, sin * step_c + cos * step_s
-
-    def table_steps(i, _):
-        for w in range(4):
-            table_step(i * 4 + w)
-        return 0
-
-    lax.fori_loop(0, 16, table_steps, 0)
+        return 0
+
+    lax.fori_loop(0, 16, table_step, 0)
 
     vis_copy.wait()
     beam_copy = pltpu.make_async_copy(beam_hbm, beam, beam_sem)
@@ -179,51 +191,64 @@
     sign = jnp.where(left, 1.0, -1.0)
     upper = (lax.broadcasted_iota(jnp.int32, (1, 8, 1), 1)) < 4
 
-    def transform(batch, _):
+    def gather(batch):
         part = r1.at[batch]
         pltpu.make_async_copy(part, part, rs1.at[batch]).wait()
         a = [r1[batch, q * 8 : (q + 1) * 8].reshape(8 * T_BLK, 2 * B_BLK).astype(F32) for q in range(4)]
         even, odd = a[0] + a[2], a[1] + a[3]
-        series[0] = (even + odd).astype(BF16)
-        series[2] = (even - odd).astype(BF16)
+        series[batch, 0] = (even + odd).astype(BF16)
+        series[batch, 2] = (even - odd).astype(BF16)
         even, odd = a[0] - a[2], sign * pltpu.roll(a[1] - a[3], B_BLK, 1)
-        series[1] = (even + odd).astype(BF16)
-        series[3] = (even - odd).astype(BF16)
+        series[batch, 1] = (even + odd).astype(BF16)
+        series[batch, 3] = (even - odd).astype(BF16)
+
+    def transform(batch, own):
         both = []
         for k in range(4):
-            along = jnp.dot(table[k], series[k], preferred_element_type=F32)
-            mixed = along[0:256] + sign * pltpu.roll(along[256:512], B_BLK, 1)
-            both.append(mixed.reshape(32, 8, 2 * B_BLK))
+            along = jnp.dot(table[k, own], series[batch, k], preferred_element_type=F32)
+            mixed = along[0:128] + sign * pltpu.roll(along[128:256], B_BLK, 1)
+            both.append(mixed.reshape(HALF // 2, 8, 2 * B_BLK))
         for p in range(2):
             first, second = both[2 * p], both[2 * p + 1]
             now = jnp.where(upper, first, pltpu.roll(second, 4, 1))
             later = jnp.where(upper, pltpu.roll(first, 4, 1), second)
             halves[:, 0, p * 8 : (p + 1) * 8, :] = now
             halves[:, 1, p * 8 : (p + 1) * 8, :] = later
-        s2[batch] = halves[...].reshape(SEGS, SEG, 2 * B_BLK).astype(BF16)
-
+        s2[batch, own] = halves[...].reshape(HALF, SEG, 2 * B_BLK).astype(BF16)
+
+    def send_spectra(batch, own):
         def send(i, _):
-            d = lax.rem(y + i // 16, 4) * 16 + lax.rem(i % 16 + (1 - half) * 8, 16)
+            to = lax.rem(g + i, HALF)
+            d = to_ma(half if own else 1 - half, to)
 
             @pl.when(d == ma)
             def _():
-                pltpu.make_async_copy(s2.at[batch, d], r2.at[batch, d], rs2.at[batch, y]).start()
+                pltpu.make_async_copy(s2.at[batch, own, to], r2.at[batch, d], rs2.at[batch, y]).start()
 
             @pl.when(d != ma)
             def _():
                 pltpu.make_async_remote_copy(
-                    src_ref=s2.at[batch, d], dst_ref=r2.at[batch, ma], send_sem=ss2, recv_sem=rs2.at[batch, y],
+                    src_ref=s2.at[batch, own, to], dst_ref=r2.at[batch, ma], send_sem=ss2, recv_sem=rs2.at[batch, y],
                     device_id=(d, af), device_id_type=MESH,
                 ).start()
 
             return 0
 
-        lax.fori_loop(0, SEGS, send, 0)
-        return 0
+        lax.fori_loop(0, HALF, send, 0)
 
     lax.fori_loop(0, 8, chunk_step, 0)
     pl.semaphore_wait(z_sem, 1)
-    lax.fori_loop(0, 2, transform, 0)
+    gather(0)
+    transform(0, 0)
+    send_spectra(0, 0)
+    transform(0, 1)
+    gather(1)
+    transform(1, 0)
+    send_spectra(1, 0)
+    send_spectra(0, 1)
+    transform(1, 1)
+    send_spectra(1, 1)
+    kl_copy.wait()
     for m in range(4):
         turned_kl[m] = kl[m].T
     weights[...] = jnp.zeros(weights.shape, BF16)
@@ -295,8 +320,8 @@
 
     sent = s1.at[:, pl.ds(0, HALF - 1)]
     pltpu.make_async_copy(sent, sent, ss1).wait()
-    sent = s2.at[:, pl.ds(0, SEGS - 1)]
-    pltpu.make_async_copy(sent, sent, ss2).wait()
+    for sent in (s2.at[:, 0], s2.at[:, 1, pl.ds(0, HALF - 1)]):
+        pltpu.make_async_copy(sent, sent, ss2).wait()
     sent = v_send.at[pl.ds(0, 3)]
     pltpu.make_async_copy(sent, sent, ssv).wait()
 
@@ -311,7 +336,7 @@
         in_specs=[
             pl.BlockSpec(memory_space=pltpu.SMEM),
             vmem,
-            vmem,
+            pl.BlockSpec(memory_space=pl.ANY),
             pl.BlockSpec(memory_space=pl.ANY),
             pl.BlockSpec(memory_space=pl.ANY),
         ],
@@ -323,18 +348,20 @@
             pltpu.VMEM((1, PADDED), jnp.int32),
             pltpu.VMEM((1, PADDED), F32),
             pltpu.VMEM((32, 2 * B_BLK), F32),
-            pltpu.VMEM((4, 512, 512), BF16),
+            pltpu.VMEM((4, 2, 256, 512), BF16),
             pltpu.VMEM((2, HALF, T_BLK, 2 * B_BLK), BF16),
             pltpu.VMEM((2, HALF, T_BLK, 2 * B_BLK), BF16),
+            pltpu.VMEM((2, 2, HALF, SEG, 2 * B_BLK), BF16),
             pltpu.VMEM((2, SEGS, SEG, 2 * B_BLK), BF16),
-            pltpu.VMEM((2, SEGS, SEG, 2 * B_BLK), BF16),
-            pltpu.VMEM((4, 512, 2 * B_BLK), BF16),
-            pltpu.VMEM((SEGS // 2, 2, SEG, 2 * B_BLK), F32),
+            pltpu.VMEM((2, 4, 512, 2 * B_BLK), BF16),
+            pltpu.VMEM((HALF // 2, 2, SEG, 2 * B_BLK), F32),
             pltpu.VMEM((2, 128, 256), BF16),
             pltpu.VMEM((2, SEG * 64, 128), F32),
             pltpu.VMEM((4, 128, 128), F32),
+            pltpu.VMEM((4, 128, 128), F32),
             pltpu.VMEM((4, 8, 128), F32),
             pltpu.VMEM((4, 8, 128), F32),
+            pltpu.SemaphoreType.DMA,
             pltpu.SemaphoreType.DMA,
             pltpu.SemaphoreType.DMA,
             pltpu.SemaphoreType.DMA,

time: 47.6 us -> 46.3 us (0.973)
  Pallas kernels: 46.9 us -> 45.5 us
    pallas_call x1, Pallas kernels: 46.9 us -> 45.5 us  [body(): pl.pallas_call(kernel, out_shape=pltpu.VMEM((4, 128), F32), in_specs=[pl....]
where the time goes in v3:
time: 46.3 us; the launch traced here: 46.1 us
  Pallas kernels  45.5 us (98%)
  local copies, waits for them, and re-layouts  0.58 us (1%)
    pallas_call x1, Pallas kernels, body(): pl.pallas_call(kernel, out_shape=pltpu.VMEM((4, 128), F32), in_specs=[pl....  45.5 us

profile of v3, /device:TPU:1, one launch (start us, length us, event | category | flops | bytes accessed | tf_op | source)
XLA Modules:
  0.0 46.1 jit_solution(13224198888773177996)
XLA Ops:
  0.0 45.5 %shard_map.55 = f32[4,128]{1,0:T(4,128)S(1)} custom-call(s32[64]{0:T(128)} %starts.1, s32[1,8160]{1,0:T(1,128)} %bitcast.5, f32[4,128,128]{2,1,0:T(8,128)} %kl_hbm.1, bf16[256,8160]{1,0:T(8,128)(2,1)} %bitcast.4, bf16[2,1024,2048]{2,1,0:T(8,128)(2,1)} %bitcast.3), custom_call_target="tpu_custom_call" | custom-call | tf_op jit(solution)/shard_map/pallas_call | solution.py:333
  45.5 0.6 %copy.7 = f32[4,128]{1,0:T(4,128)} copy(f32[4,128]{1,0:T(4,128)S(1)} %shard_map.55) | data formatting | bytes 4096

commit v4 on v3

--- a/solution.py
+++ b/solution.py
@@ -31,8 +31,8 @@
 NT = (((1,), (1,)), ((), ()))
 
 
-def to_ma(half, g):
-    return (g // 8) * 16 + half * 8 + g % 8
+def wrap(value, size):
+    return jnp.where(value >= size, value - size, value)
 
 
 def sincos(phase):
@@ -58,9 +58,10 @@
     af = lax.axis_index("af")
     y = ma // 16
     half = (ma // 8) % 2
-    g = y * 8 + ma % 8
-    x = (g // 2) % 4
-    partner = to_ma(1 - half, g)
+    place = ma % 8
+    g = y * 8 + place
+    x = place // 2
+    partner = ma + 8 - 16 * half
 
     vis_copy = pltpu.make_async_copy(vis_hbm, vis, vis_sem)
     vis_copy.start()
@@ -70,14 +71,16 @@
     barrier = pltpu.get_barrier_semaphore()
     pl.semaphore_signal(barrier, inc=1, device_id=(partner, af), device_id_type=MESH)
 
-    def greet(k, _):
-        pl.semaphore_signal(barrier, inc=1, device_id=(to_ma(half, lax.rem(g + k, HALF)), af), device_id_type=MESH)
-        return 0
-
-    lax.fori_loop(1, HALF, greet, 0)
+    for dy in range(4):
+
+        def greet(k, _, base=wrap(y + dy, 4) * 16 + half * 8):
+            pl.semaphore_signal(barrier, inc=1, device_id=(base + wrap(place + k, 8), af), device_id_type=MESH)
+            return 0
+
+        lax.fori_loop(0 if dy else 1, 8, greet, 0)
 
     def greet_af(k, _):
-        pl.semaphore_signal(barrier, inc=1, device_id=(ma, lax.rem(af + k, 4)), device_id_type=MESH)
+        pl.semaphore_signal(barrier, inc=1, device_id=(ma, wrap(af + k, 4)), device_id_type=MESH)
         return 0
 
     lax.fori_loop(1, 4, greet_af, 0)
@@ -141,15 +144,17 @@
     left = lane < B_BLK
 
     def chunk_step(k, _):
-        batch = k // 4
-        n = k % 4
+        batch = jnp.where(k >= 4, 1, 0)
+        n = k - 4 * batch
         chips = []
+        places = []
         for sub in range(4):
             dx = dy = 0
             for i in range(4):
                 dx = jnp.where(n == i, OFFSETS[i][sub][0], dx)
                 dy = jnp.where(n == i, OFFSETS[i][sub][1], dy)
-            chips.append(lax.rem(y + dy, 4) * 4 + lax.rem(x + dx, 4))
+            chips.append(wrap(y + dy, 4) * 4 + wrap(x + dx, 4))
+            places.append(wrap(y + dy, 4) * 16 + half * 8 + wrap(x + dx, 4) * 2)
         wanted = jnp.full((1, PADDED), -1.0, F32)
         for sub in range(4):
             wanted = jnp.where(high[...] == batch * 16 + chips[sub], low[...] + (sub * B_BLK), wanted)
@@ -175,16 +180,20 @@
             for c in range(2):
                 d = chips[sub] * 2 + c
 
-                @pl.when(d == g)
-                def _():
-                    pltpu.make_async_copy(s1.at[batch, d], r1.at[batch, d], rs1.at[batch]).start()
-
-                @pl.when(d != g)
-                def _():
+                def send(d=d, to=places[sub] + c):
                     pltpu.make_async_remote_copy(
                         src_ref=s1.at[batch, d], dst_ref=r1.at[batch, g], send_sem=ss1, recv_sem=rs1.at[batch],
-                        device_id=(to_ma(half, d), af), device_id_type=MESH,
+                        device_id=(to, af), device_id_type=MESH,
                     ).start()
+
+                if sub < 3:
+                    send()
+                else:
+                    pl.when(d != g)(send)
+
+                    @pl.when(d == g)
+                    def _():
+                        pltpu.make_async_copy(s1.at[batch, d], r1.at[batch, d], rs1.at[batch]).start()
 
         return 0
 
@@ -217,24 +226,20 @@
         s2[batch, own] = halves[...].reshape(HALF, SEG, 2 * B_BLK).astype(BF16)
 
     def send_spectra(batch, own):
-        def send(i, _):
-            to = lax.rem(g + i, HALF)
-            d = to_ma(half if own else 1 - half, to)
-
-            @pl.when(d == ma)
-            def _():
-                pltpu.make_async_copy(s2.at[batch, own, to], r2.at[batch, d], rs2.at[batch, y]).start()
-
-            @pl.when(d != ma)
-            def _():
+        for dy in range(4):
+            other = wrap(y + dy, 4)
+
+            def send(k, _, other=other):
+                near = wrap(place + k, 8)
                 pltpu.make_async_remote_copy(
-                    src_ref=s2.at[batch, own, to], dst_ref=r2.at[batch, ma], send_sem=ss2, recv_sem=rs2.at[batch, y],
-                    device_id=(d, af), device_id_type=MESH,
+                    src_ref=s2.at[batch, own, other * 8 + near], dst_ref=r2.at[batch, ma], send_sem=ss2, recv_sem=rs2.at[batch, y],
+                    device_id=(other * 16 + (half if own else 1 - half) * 8 + near, af), device_id_type=MESH,
                 ).start()
-
-            return 0
-
-        lax.fori_loop(0, HALF, send, 0)
+                return 0
+
+            lax.fori_loop(1 if own and not dy else 0, 8, send, 0)
+        if own:
+            pltpu.make_async_copy(s2.at[batch, 1, g], r2.at[batch, ma], rs2.at[batch, y]).start()
 
     lax.fori_loop(0, 8, chunk_step, 0)
     pl.semaphore_wait(z_sem, 1)
@@ -259,8 +264,8 @@
     beam_copy.wait()
 
     def project_step(k, _):
-        batch = k // 4
-        q = lax.rem(y - k % 4 + 4, 4)
+        batch = jnp.where(k >= 4, 1, 0)
+        q = wrap(y - (k - 4 * batch) + 4, 4)
         part = r2.at[batch, pl.ds(q * 16, 16)]
         pltpu.make_async_copy(part, part, rs2.at[batch, q]).wait()
         for c in range(2):
@@ -304,7 +309,7 @@
     pltpu.make_async_copy(v_send.at[af], v_recv.at[af], rsv).start()
 
     def send_sky(k, _):
-        a = lax.rem(af + k, 4)
+        a = wrap(af + k, 4)
         pltpu.make_async_remote_copy(
             src_ref=v_send.at[a], dst_ref=v_recv.at[af], send_sem=ssv, recv_sem=rsv,
             device_id=(ma, a), device_id_type=MESH,

time: 46.3 us -> 45.4 us (0.981)
  Pallas kernels: 45.5 us -> 44.6 us
    pallas_call x1, Pallas kernels: 45.5 us -> 44.6 us  [body(): pl.pallas_call(kernel, out_shape=pltpu.VMEM((4, 128), F32), in_specs=[pl....]
where the time goes in v4:
time: 45.4 us; the launch traced here: 45.2 us
  Pallas kernels  44.6 us (98%)
  local copies, waits for them, and re-layouts  0.58 us (1%)
    pallas_call x1, Pallas kernels, body(): pl.pallas_call(kernel, out_shape=pltpu.VMEM((4, 128), F32), in_specs=[pl....  44.6 us

profile of v4, /device:TPU:1, one launch (start us, length us, event | category | flops | bytes accessed | tf_op | source)
XLA Modules:
  0.0 45.2 jit_solution(15649423545259855861)
XLA Ops:
  0.0 44.6 %shard_map.55 = f32[4,128]{1,0:T(4,128)S(1)} custom-call(s32[64]{0:T(128)} %starts.1, s32[1,8160]{1,0:T(1,128)} %bitcast.5, f32[4,128,128]{2,1,0:T(8,128)} %kl_hbm.1, bf16[256,8160]{1,0:T(8,128)(2,1)} %bitcast.4, bf16[2,1024,2048]{2,1,0:T(8,128)(2,1)} %bitcast.3), custom_call_target="tpu_custom_call" | custom-call | tf_op jit(solution)/shard_map/pallas_call | solution.py:338
  44.6 0.6 %copy.7 = f32[4,128]{1,0:T(4,128)} copy(f32[4,128]{1,0:T(4,128)S(1)} %shard_map.55) | data formatting | bytes 4096

commit v5 on v4

--- a/solution.py
+++ b/solution.py
@@ -160,8 +160,8 @@
             wanted = jnp.where(high[...] == batch * 16 + chips[sub], low[...] + (sub * B_BLK), wanted)
         rows = lax.broadcasted_iota(jnp.int32, (CHUNK, PADDED), 0).astype(BF16)
         one = jnp.where(rows == jnp.broadcast_to(wanted.astype(BF16), (CHUNK, PADDED)), BF16(1), BF16(0))
-        sums = lax.dot_general(vis[:, pl.ds(0, WHOLE)], one[:, :WHOLE], NT, preferred_element_type=F32)
-        sums += lax.dot_general(tail[...], one[:, WHOLE:], NT, preferred_element_type=F32)
+        pairs = jnp.concatenate([vis[:, pl.ds(0, WHOLE)], tail[...]], axis=1)
+        sums = lax.dot_general(pairs, one, NT, preferred_element_type=F32)
         for pair in range(2):
             near, far = chips[pair * 2], chips[pair * 2 + 1]
             scale = 1.0 / jnp.where(left, counts[pl.ds(batch * 16 + near, 1), :], counts[pl.ds(batch * 16 + far, 1), :])

time: 45.4 us -> 45.4 us (level)
  no operation moved by 1% of the time
where the time goes in v5:
time: 45.4 us; the launch traced here: 45.2 us
  Pallas kernels  44.6 us (98%)
  local copies, waits for them, and re-layouts  0.58 us (1%)
    pallas_call x1, Pallas kernels, body(): pl.pallas_call(kernel, out_shape=pltpu.VMEM((4, 128), F32), in_specs=[pl....  44.6 us

profile of v5, /device:TPU:1, one launch (start us, length us, event | category | flops | bytes accessed | tf_op | source)
XLA Modules:
  0.0 45.2 jit_solution(3691111642508107306)
XLA Ops:
  0.0 44.6 %shard_map.55 = f32[4,128]{1,0:T(4,128)S(1)} custom-call(s32[64]{0:T(128)} %starts.1, s32[1,8160]{1,0:T(1,128)} %bitcast.5, f32[4,128,128]{2,1,0:T(8,128)} %kl_hbm.1, bf16[256,8160]{1,0:T(8,128)(2,1)} %bitcast.4, bf16[2,1024,2048]{2,1,0:T(8,128)(2,1)} %bitcast.3), custom_call_target="tpu_custom_call" | custom-call | tf_op jit(solution)/shard_map/pallas_call | solution.py:338
  44.6 0.6 %copy.7 = f32[4,128]{1,0:T(4,128)} copy(f32[4,128]{1,0:T(4,128)S(1)} %shard_map.55) | data formatting | bytes 4096
